TPU v7x, 128 devices: a whole 4x4x4 slice. The times are simulated.
128 devices in a mesh: tm: 8 (over y, core), row: 8 (over z_lo, x), col: 2 (over z_hi).
Axes of the slice: x: 4, y: 4, z: 4 (z_hi: 2, z_lo: 2; z = z_hi * 2 + z_lo), core: 2. Of those that a mesh axis runs over, the one named last changes fastest.
Arguments:
- paths: bfloat16 [8, 1024, 6144], P('tm', 'row', 'col'), may hold values from -18 to 18
- prev_drift: bfloat16 [8, 1024, 6144], P('tm', 'row', 'col'), may hold values from -6 to 6
- boundary: bfloat16 [2, 1024, 6144], P(None, 'row', 'col'), may hold values from -6 to 6
- step_scale: float32 [8], P('tm'), may hold values from 0.3 to 3
- time_ids: int32 [8], P('tm'), may hold values from 0 to 63
- mod_table: bfloat16 [64, 2, 6144], P(None, None, 'col'), may hold values from -1.796875 to 1.796875
- w_qkv: bfloat16 [6144, 3, 3072], P('col', None, 'row'), may hold values from -2 to 2
- output_weight: bfloat16 [3072, 6144], P('row', 'col'), may hold values from -0.109375 to 0.109375
Outputs:
- grad_w_qkv: float32 [6144, 3, 3072], P(('col', 'tm'), None, 'row')
- grad_w_out: float32 [3072, 6144], P('row', ('col', 'tm'))
All inputs are finite; a program needn't handle non-finite values.
Results may differ from a plain program's by a relative error of at most 0.013.
Values may be sent and summed in bfloat16 or wider, within the bound.
A program may use at most 128 MiB of HBM per device.

v0:
```python
import jax
import jax.numpy as jnp
from jax import lax
from jax.sharding import PartitionSpec as P

D = 6144
HEAD_DIM = 128
NT = 64


norm_eps = 1e-06


def shifted(array, axis, by):
    count = lax.axis_size(axis)
    pairs = [(i, i + by) for i in range(count) if 0 <= i + by < count]
    return lax.ppermute(array, axis, pairs)


def attend_head(operands):
    query_rows, key_rows, value_rows = operands
    scores = jnp.dot(query_rows, key_rows.T, preferred_element_type=jnp.float32) * HEAD_DIM ** (
        -0.5
    )
    weights = jax.nn.softmax(scores, axis=-1)
    weights_low = weights.astype(jnp.bfloat16)
    mixed_rows = jnp.dot(weights_low, value_rows, preferred_element_type=jnp.float32).astype(
        jnp.bfloat16
    )
    return (mixed_rows, weights)


def head_grads(operands):
    query_rows, key_rows, value_rows, weights, upstream = operands
    weights_low = weights.astype(jnp.bfloat16)
    grad_value = jnp.dot(weights_low.T, upstream, preferred_element_type=jnp.float32).astype(
        jnp.bfloat16
    )
    grad_weights = jnp.dot(upstream, value_rows.T, preferred_element_type=jnp.float32)
    inner_sum = jnp.sum(grad_weights * weights, axis=-1, keepdims=True)
    grad_scores = (weights * (grad_weights - inner_sum) * HEAD_DIM ** (-0.5)).astype(jnp.bfloat16)
    grad_query = jnp.dot(grad_scores, key_rows, preferred_element_type=jnp.float32).astype(
        jnp.bfloat16
    )
    grad_key = jnp.dot(grad_scores.T, query_rows, preferred_element_type=jnp.float32).astype(
        jnp.bfloat16
    )
    return (grad_query, grad_key, grad_value)


def body(paths, prev_drift, boundary, step_scale, time_ids, mod_table, w_qkv, output_weight):
    step_count, tok_rows, feat_cols = paths.shape
    local_width = output_weight.shape[0]
    local_heads = local_width // HEAD_DIM
    seq_len = tok_rows * lax.axis_size("row")
    moved_state, moved_drift = shifted((paths[step_count - 1], prev_drift[step_count - 1]), "tm", 1)
    at_start = lax.axis_index("tm") == 0
    start_state = jnp.where(at_start, boundary[0], moved_state)
    start_drift = jnp.where(at_start, boundary[1], moved_drift)
    prev_states = jnp.concatenate([start_state[None], paths[: step_count - 1]], axis=0)
    prev_drifts = jnp.concatenate([start_drift[None], prev_drift[: step_count - 1]], axis=0)
    targets = prev_states.astype(jnp.float32) + step_scale[:, None, None] * (
        prev_drifts.astype(jnp.float32) - prev_drift.astype(jnp.float32)
    )
    onehot = (time_ids[:, None] == jnp.arange(NT)[None, :]).astype(jnp.float32)
    modulation = jnp.dot(
        onehot,
        mod_table.reshape(NT, 2 * feat_cols).astype(jnp.float32),
        precision=lax.Precision.HIGHEST,
    ).reshape(step_count, 2, feat_cols)
    state_f = paths.astype(jnp.float32)
    square_sums = lax.psum(jnp.sum(state_f * state_f, axis=-1), "col")
    scale_rows = lax.rsqrt(square_sums / D + norm_eps)[..., None]
    normed = (state_f * scale_rows * (1.0 + modulation[:, 0:1, :]) + modulation[:, 1:2, :]).astype(
        jnp.bfloat16
    )
    flattened_weight = w_qkv.reshape(feat_cols, 3 * local_width)
    collected_rows = lax.all_gather(normed, "row", axis=1, tiled=True)
    partial_query_key_value = jnp.einsum(
        "pbu,um->pbm", collected_rows, flattened_weight, preferred_element_type=jnp.float32
    )
    projected = lax.psum(partial_query_key_value, "col").astype(jnp.bfloat16)
    heads_first = jnp.transpose(
        projected.reshape(step_count, seq_len, 3, local_heads, HEAD_DIM), (2, 0, 3, 1, 4)
    ).reshape(3, step_count * local_heads, seq_len, HEAD_DIM)
    mixed_heads, weights = lax.map(attend_head, (heads_first[0], heads_first[1], heads_first[2]))
    mixed_rows = jnp.transpose(
        mixed_heads.reshape(step_count, local_heads, seq_len, HEAD_DIM), (2, 0, 1, 3)
    ).reshape(seq_len, step_count, local_width)
    attention_block = mixed_rows
    mix_out = lax.psum_scatter(
        jnp.einsum(
            "lsh,hd->lsd", attention_block, output_weight, preferred_element_type=jnp.float32
        ).astype(jnp.bfloat16),
        "row",
        scatter_dimension=0,
        tiled=True,
    ).astype(jnp.float32)
    output = state_f + jnp.transpose(mix_out, (1, 0, 2))
    upstream = ((output - targets) * seq_len ** (-0.5)).astype(jnp.bfloat16)
    slice_rows = lax.all_gather(upstream, "row", axis=1, tiled=True)
    attention_block = mixed_rows
    output_gradient = jnp.einsum(
        "uqw,quc->wc", attention_block, slice_rows, preferred_element_type=jnp.float32
    )
    slice_gradient = jnp.einsum(
        "ujf,nf->jun", slice_rows, output_weight, preferred_element_type=jnp.float32
    )
    output_gradient, grad_partial = (output_gradient, slice_gradient)
    grad_mixed = lax.psum(grad_partial.astype(jnp.bfloat16), "col")
    grad_heads = jnp.transpose(
        grad_mixed.reshape(seq_len, step_count, local_heads, HEAD_DIM), (1, 2, 0, 3)
    ).reshape(step_count * local_heads, seq_len, HEAD_DIM)
    grad_query, grad_key, grad_value = lax.map(
        head_grads, (heads_first[0], heads_first[1], heads_first[2], weights, grad_heads)
    )
    grad_stack = jnp.stack([grad_query, grad_key, grad_value]).reshape(
        3, step_count, local_heads, seq_len, HEAD_DIM
    )
    query_key_value_gradient = jnp.transpose(grad_stack, (1, 3, 0, 2, 4)).reshape(
        step_count, seq_len, 3 * local_width
    )
    input_gradient = jnp.einsum(
        "nbr,nbf->rf", collected_rows, query_key_value_gradient, preferred_element_type=jnp.float32
    )
    grad_in_sum = lax.psum_scatter(
        input_gradient.reshape(feat_cols, 3, local_width).astype(jnp.bfloat16),
        "tm",
        scatter_dimension=0,
        tiled=True,
    ).astype(jnp.float32)
    grad_out_sum = lax.psum_scatter(
        output_gradient.astype(jnp.bfloat16), "tm", scatter_dimension=1, tiled=True
    ).astype(jnp.float32)
    return (grad_in_sum, grad_out_sum)


def solution(mesh):
    placed = (
        P("tm", "row", "col"),
        P("tm", "row", "col"),
        P(None, "row", "col"),
        P("tm"),
        P("tm"),
        P(None, None, "col"),
        P("col", None, "row"),
        P("row", "col"),
    )
    return jax.shard_map(
        body,
        mesh=mesh,
        in_specs=placed,
        out_specs=(P(("col", "tm"), None, "row"), P("row", ("col", "tm"))),
        check_vma=False,
    )
```

profile of v0, /device:TPU:1, one launch (start us, length us, event | category | flops | bytes accessed | tf_op | source)
XLA Modules:
  0.0 587.2 jit_solution(1015838862860359904)
XLA Ops:
  10.9 6.7 %psum.21 = f32[1,128]{1,0:T(1,128)S(1)} all-reduce(f32[1,128]{1,0:T(1,128)S(1)} %bitcast.231), channel_id=1, replica_groups=mesh['tm'=8,'row'=8,'col'=2] {'col'}, use_global_device_ids=true, to_apply=%region_1.2 | all-reduce | flops 128 | bytes 1024 | tf_op jit(solution)/shard_map/psum | solution.py:72
  17.6 2.3 fusion.70
  20.0 10.3 %copy.27 = bf16[3072,3,384]{0,2,1:T(8,128)(2,1)} copy(bf16[3072,3,384]{2,0,1:T(8,128)(2,1)} %param.18) | data formatting | bytes 14155776 | tf_op args[6]
  30.3 65.0 %all-gather.3.cloned.1.call-done = bf16[1,1024,3072]{2,1,0:T(8,128)(2,1)} async-done(((bf16[1,128,3072]{2,1,0:T(8,128)(2,1)}), bf16[1,1024,3072]{2,1,0:T(8,128)(2,1)}) %all-gather.3.cloned.1.call-update) | async-done | bytes 6291472 | tf_op jit(solution)/shard_map/all_gather | solution.py:78
  95.3 14.0 %fusion.61 = f32[1,1024,1152]{2,1,0:T(8,128)} fusion(bf16[3072,1152]{0,1:T(8,128)(2,1)} %bitcast.217, bf16[1,1024,3072]{2,1,0:T(8,128)(2,1)} %all-gather.3.cloned.1.call-done), kind=kOutput, calls=%fused_computation.62 | convolution fusion | flops 7247757312 | bytes 18087936 | tf_op jit(solution)/shard_map/pbu,um->pbm/dot_general | solution.py:79
  109.4 113.9 %all-reduce.4 = bf16[1,1024,1152]{2,1,0:T(8,128)(2,1)} all-reduce(f32[1,1024,1152]{2,1,0:T(8,128)} %fusion.61), channel_id=1, replica_groups=mesh['tm'=8,'row'=8,'col'=2] {'col'}, use_global_device_ids=true, to_apply=%region_2.3 | all-reduce | flops 1179648 | bytes 7077888 | tf_op jit(solution)/shard_map/psum | solution.py:82
  223.3 4.3 copy.28
  227.5 3.1 slice_bitcast_fusion
  232.1 2.3 copy.30
  234.5 2.3 copy.31
  237.7 29.0 %while.26 = (s32[]{:T(128)}, bf16[3,1024,128]{1,2,0:T(8,128)(2,1)}, f32[3,1024,1024]{1,2,0:T(8,128)}, bf16[3,1024,128]{2,1,0:T(8,128)(2,1)S(1)}, bf16[3,1024,128...) while((s32[]{:T(128)}, bf16[3,1024,128]{1,2,0:T(8,128)(2,1)}, f32[3,1024,1024]{1,2,0:T(8,128)}, ...), condition=%wide.region_6.7_spmd, body=%wide.region_3.6_spmd.sunk | while | flops 549582848 | bytes 23099980 | solution.py:86
  237.7 1.7 multiply_reduce_fusion.2
  240.1 2.7 bitcast_dynamic-update-slice_fusion.2
  242.8 2.8 fusion.113
  249.8 2.7 bitcast_dynamic-update-slice_fusion.2
  252.5 2.8 fusion.113
  259.5 2.7 bitcast_dynamic-update-slice_fusion.2
  262.2 2.8 fusion.113
  266.8 6.7 %convert_bitcast_fusion = bf16[1024,1,3072]{2,0,1:T(8,128)(2,1)} fusion(bf16[1024,384]{0,1:T(8,128)(2,1)} %bitcast.225, bf16[384,3072]{1,0:T(8,128)(2,1)S(1)} %copy-done), kind=kOutput, calls=%fused_computation.60 | convolution fusion | flops 2419064832 | bytes 9437184 | tf_op jit(solution)/shard_map/lsh,hd->lsd/dot_general | solution.py:92
  273.6 5.2 collective-permute-start
  278.8 2.1 collective-permute-start.1
  281.5 6.5 %collective-permute-done = bf16[128,3072]{1,0:T(8,128)(2,1)} collective-permute-done((bf16[128,3072]{1,0:T(8,128)(2,1)}, bf16[128,3072]{1,0:T(8,128)(2,1)}, u32[]{:S(2)}, u32[]{:S(2)}) %collective-permute-start) | collective-permute-done | bytes 786464 | tf_op jit(solution)/shard_map/ppermute | solution.py:17
  288.0 8.4 %collective-permute-done.1 = bf16[128,3072]{1,0:T(8,128)(2,1)} collective-permute-done((bf16[128,3072]{1,0:T(8,128)(2,1)}, bf16[128,3072]{1,0:T(8,128)(2,1)}, u32[]{:S(2)}, u32[]{:S(2)}) %collective-permute-start.1) | collective-permute-done | bytes 786464 | tf_op jit(solution)/shard_map/ppermute | solution.py:17
  296.4 48.6 %reduce-scatter.6.cloned.1.call-done = bf16[128,1,3072]{2,0,1:T(8,128)(2,1)} async-done(((bf16[1024,1,3072]{2,0,1:T(8,128)(2,1)}), bf16[128,1,3072]{2,0,1:T(8,128)(2,1)}) %reduce-scatter.6.cloned.1.call-update) | async-done | bytes 786448 | tf_op jit(solution)/shard_map/reduce_scatter | solution.py:91
  345.1 4.3 fusion.73
  349.5 71.1 %all-gather.5.cloned.1.call-done = bf16[1,1024,3072]{2,1,0:T(8,128)(2,1)} async-done(((bf16[1,128,3072]{2,1,0:T(8,128)(2,1)}), bf16[1,1024,3072]{2,1,0:T(8,128)(2,1)}) %all-gather.5.cloned.1.call-update) | async-done | bytes 6291472 | tf_op jit(solution)/shard_map/all_gather | solution.py:101
  420.6 6.3 %fusion.76 = bf16[1024,384]{0,1:T(8,128)(2,1)} fusion(bf16[384,3072]{1,0:T(8,128)(2,1)S(1)} %copy-done, bf16[1,1024,3072]{2,1,0:T(8,128)(2,1)} %all-gather.5.cloned.1.call-done), kind=kOutput, calls=%fused_computation.78 | convolution fusion | flops 2416312320 | bytes 9437184 | tf_op jit(solution)/shard_map/ujf,nf->jun/dot_general | solution.py:106
  426.9 2.3 copy.33
  429.3 5.6 fusion.64
  434.9 2.5 copy.45
  437.5 33.1 %all-reduce.3.cloned.1.call-done = bf16[3,1024,128]{2,1,0:T(8,128)(2,1)} async-done(((bf16[3,1024,128]{2,1,0:T(8,128)(2,1)}), bf16[3,1024,128]{2,1,0:T(8,128)(2,1)}) %all-reduce.3.cloned.1.call-update) | async-done | bytes 786448 | tf_op jit(solution)/shard_map/psum | solution.py:110
  473.5 42.6 %while.27 = (s32[]{:T(128)}, bf16[3,1024,128]{1,2,0:T(8,128)(2,1)}, bf16[3,1024,128]{1,2,0:T(8,128)(2,1)}, bf16[3,1024,128]{1,2,0:T(8,128)(2,1)}, f32[3,1024,102...) while((s32[]{:T(128)}, bf16[3,1024,128]{1,2,0:T(8,128)(2,1)}, ...), condition=%wide.region_11.12_spmd, body=%wide.region_9.11_spmd.sunk | while | flops 1080425472 | bytes 36712612 | solution.py:114
  473.5 3.3 fusion.120
  476.9 3.3 fusion.121
  481.1 2.9 fusion.123
  485.0 1.8 fusion.122
  487.7 3.4 fusion.120
  491.0 3.3 fusion.121
  495.2 3.0 fusion.123
  499.2 1.8 fusion.122
  501.9 3.4 fusion.120
  505.3 3.3 fusion.121
  509.5 2.9 fusion.123
  513.4 1.8 fusion.122
  516.1 1.9 pad_maximum_fusion
  518.0 14.7 %fusion.58 = bf16[3072,3,384]{2,0,1:T(8,128)(2,1)} fusion(bf16[3,384,1024]{2,1,0:T(8,128)(2,1)S(1)} %bitcast.223, bf16[1,1024,3072]{2,1,0:T(8,128)(2,1)} %all-gather.3.cloned.1.call-done), kind=kOutput, calls=%fused_computation.61 | convolution fusion | flops 7251296256 | bytes 15728640 | tf_op jit(solution)/shard_map/nbr,nbf->rf/dot_general | solution.py:123
  534.9 43.0 %reduce-scatter.8.cloned.1.call-done = bf16[384,3,384]{2,0,1:T(8,128)(2,1)} async-done(((bf16[3072,3,384]{2,0,1:T(8,128)(2,1)}), bf16[384,3,384]{2,0,1:T(8,128)(2,1)}) %reduce-scatter.8.cloned.1.call-update) | async-done | bytes 884752 | tf_op jit(solution)/shard_map/reduce_scatter | solution.py:126
  577.9 2.5 convert_element_type.100
  (71 shorter events, 30.0 us)
Async XLA Ops:
  7.2 259.6 %copy-start = (bf16[384,3072]{1,0:T(8,128)(2,1)S(1)}, bf16[384,3072]{1,0:T(8,128)(2,1)}, u32[]{:S(2)}) copy-start(bf16[384,3072]{1,0:T(8,128)(2,1)} %param.19) | copy-start | bytes 7077892
  7.2 88.2 %all-gather.3.cloned.1.call-start = ((), (), s32[]{:S(2)}) async-start(), calls=%async_computation.3 | async-start | bytes 7077888 | tf_op jit(solution)/shard_map/all_gather | solution.py:78
  20.0 325.1 %reduce-scatter.6.cloned.1.call-start = ((), (), s32[]{:S(2)}) async-start(), calls=%async_computation.4 | async-start | bytes 7077888 | tf_op jit(solution)/shard_map/reduce_scatter | solution.py:91
  273.5 147.1 %all-gather.5.cloned.1.call-start = ((), (), s32[]{:S(2)}) async-start(), calls=%async_computation.5 | async-start | bytes 7077888 | tf_op jit(solution)/shard_map/all_gather | solution.py:101
  273.6 14.4 %collective-permute-start = (bf16[128,3072]{1,0:T(8,128)(2,1)}, bf16[128,3072]{1,0:T(8,128)(2,1)}, u32[]{:S(2)}, u32[]{:S(2)}) collective-permute-start(bf16[128,3072]{1,0:T(8,128)(2,1)} %bitcast.218), channel_id=1, source_target_pairs={{0,16},{16,32},{32,48},{48,64},{64,80},{80,96},{96,112},{1,17},{17... | collective-permute-start | bytes 2359304 | tf_op jit(solution)/shard_map/ppermute | solution.py:17
  278.8 17.7 %collective-permute-start.1 = (bf16[128,3072]{1,0:T(8,128)(2,1)}, bf16[128,3072]{1,0:T(8,128)(2,1)}, u32[]{:S(2)}, u32[]{:S(2)}) collective-permute-start(bf16[128,3072]{1,0:T(8,128)(2,1)} %bitcast.227), channel_id=1, source_target_pairs={{0,16},{16,32},{32,48},{48,64},{64,80},{80,96},{96,112},{1,17},{17... | collective-permute-start | bytes 2359304 | tf_op jit(solution)/shard_map/ppermute | solution.py:17
  349.4 121.1 %all-reduce.3.cloned.1.call-start = ((), (), s32[]{:S(2)}) async-start(), calls=%async_computation.6 | async-start | bytes 1572864 | tf_op jit(solution)/shard_map/psum | solution.py:110
  429.2 103.5 %reduce-scatter.10.cloned.1.call-start = ((), (), s32[]{:S(2)}) async-start(), calls=%async_computation.8 | async-start | bytes 2654208
  437.4 140.5 %reduce-scatter.8.cloned.1.call-start = ((), (), s32[]{:S(2)}) async-start(), calls=%async_computation.7 | async-start | bytes 7962624 | tf_op jit(solution)/shard_map/reduce_scatter | solution.py:126
  473.5 6.6 %copy-start.2 = (bf16[3,1024,128]{2,1,0:T(8,128)(2,1)}, bf16[3,1024,128]{2,1,0:T(8,128)(2,1)S(1)}, u32[]{:S(2)}) copy-start(bf16[3,1024,128]{2,1,0:T(8,128)(2,1)S(1)} %get-tuple-element.311) | copy-start | bytes 2359300 | tf_op jit(solution)/shard_map/while
  485.0 2.7 copy-start.3
  487.7 6.7 %copy-start.2 = (bf16[3,1024,128]{2,1,0:T(8,128)(2,1)}, bf16[3,1024,128]{2,1,0:T(8,128)(2,1)S(1)}, u32[]{:S(2)}) copy-start(bf16[3,1024,128]{2,1,0:T(8,128)(2,1)S(1)} %get-tuple-element.311) | copy-start | bytes 2359300 | tf_op jit(solution)/shard_map/while
  499.2 2.7 copy-start.3
  501.9 6.7 %copy-start.2 = (bf16[3,1024,128]{2,1,0:T(8,128)(2,1)}, bf16[3,1024,128]{2,1,0:T(8,128)(2,1)S(1)}, u32[]{:S(2)}) copy-start(bf16[3,1024,128]{2,1,0:T(8,128)(2,1)S(1)} %get-tuple-element.311) | copy-start | bytes 2359300 | tf_op jit(solution)/shard_map/while
  513.4 2.7 copy-start.3
  532.7 47.7 %copy-start.1 = (bf16[384,3072]{1,0:T(8,128)(2,1)S(1)}, bf16[384,3072]{1,0:T(8,128)(2,1)}, u32[]{:S(2)}) copy-start(bf16[384,3072]{1,0:T(8,128)(2,1)} %param.19) | copy-start | bytes 7077892
Sparse Core Ops, SparseCore 0:
  20.1 75.2 all-gather.2
  273.6 71.3 reduce-scatter.5
  349.6 70.9 all-gather.4
  429.4 41.1 all-reduce.2
  473.0 30.3 reduce-scatter.9
  532.9 44.9 reduce-scatter.7
where the time goes:
time: 589 us; the launch traced here: 587 us
  waiting for transfers between devices  276 us (47%)
  blocking collectives  121 us (21%)
  matrix products  88.7 us (15%)
  local copies, waits for them, and re-layouts  45.3 us (8%)
  other arithmetic  33.4 us (6%)
  between operations  15.7 us (3%)
  starting transfers between devices  7.54 us (1%)
    psum x1, blocking collectives, body(): projected = lax.psum(partial_query_key_value, 'col').astype(jnp.bfloat16)  114 us
    all_gather x1, waiting for transfers between devices, body(): slice_rows = lax.all_gather(upstream, 'row', axis=1, tiled=True)  71.1 us
    all_gather x1, waiting for transfers between devices, body(): collected_rows = lax.all_gather(normed, 'row', axis=1, tiled=True)  65 us
    reduce_scatter x1, waiting for transfers between devices, body(): lax.psum_scatter(jnp.einsum('lsh,hd->lsd', attention_block, output_weight...  48.6 us
    reduce_scatter x1, waiting for transfers between devices, body(): lax.psum_scatter(input_gradient.reshape(feat_cols, 3, local_width).astype...  43 us
    psum x1, waiting for transfers between devices, body(): grad_mixed = lax.psum(grad_partial.astype(jnp.bfloat16), 'col')  33.1 us
    ppermute x2, waiting for transfers between devices, shifted(): return lax.ppermute(array, axis, pairs)  14.9 us
    dot_general x1, matrix products, body(): jnp.einsum('nbr,nbf->rf', collected_rows, query_key_value_gradient, prefe...  14.7 us
  transfers between devices with their start and end apart: 8, of which 7 were waited for; matrix products, arithmetic and copies ran while one was open for 14% of the time, Pallas kernels for 0%

commit v1 on v0

v1 whole, which is shorter than its diff:
```python
import jax
import jax.numpy as jnp
from jax import lax
from jax.experimental import pallas as pl
from jax.experimental.pallas import tpu as pltpu
from jax.sharding import PartitionSpec as P

D = 6144
HEAD_DIM = 128
SCALE = HEAD_DIM**-0.5
MESH = pl.DeviceIdType.MESH
VMEM_LIMIT = 60 * 1024 * 1024

norm_eps = 1e-06

BF16 = jnp.bfloat16
F32 = jnp.float32


class Place:
    def __init__(self):
        self.t = lax.axis_index("tm")
        self.r = lax.axis_index("row")
        self.c = lax.axis_index("col")
        x = lax.rem(self.r, 4)
        base = self.r - x
        other = lax.rem(base + 4, 8)
        self.left = base + lax.rem(x + 3, 4)
        self.right = base + lax.rem(x + 1, 4)
        self.far = base + lax.rem(x + 2, 4)
        self.z = other + x
        self.zleft = other + lax.rem(x + 3, 4)
        self.zright = other + lax.rem(x + 1, 4)
        self.zfar = other + lax.rem(x + 2, 4)

    def row(self, r):
        return (self.t, r, self.c)

    def col(self):
        return (self.t, self.r, 1 - self.c)


def greet(signalled, awaited):
    barrier = pltpu.get_barrier_semaphore()
    for device in signalled:
        pl.semaphore_signal(barrier, inc=1, device_id=device, device_id_type=MESH)
    pl.semaphore_wait(barrier, awaited)


def remote(src, dst, send_sem, recv_sem, device):
    return pltpu.make_async_remote_copy(
        src_ref=src,
        dst_ref=dst,
        send_sem=send_sem,
        recv_sem=recv_sem,
        device_id=device,
        device_id_type=MESH,
    )


class Gather:
    def __init__(self, place, buf, send_sems, recv_sems, far_over_z):
        p = place
        low, high, full = pl.ds(0, 64), pl.ds(64, 64), pl.ds(0, 128)
        plan = [
            (p.r, p.left, full, p.right),
            (p.r, p.right, full, p.left),
            (p.r, p.z, full, p.z),
            (p.left, p.far, low, p.right),
            (p.right, p.far, high, p.left),
            (p.z, p.zleft, full, p.right),
            (p.z, p.zright, full, p.left),
        ]
        if far_over_z:
            plan += [(p.far, p.zfar, full, p.z)]
        else:
            plan += [(p.zleft, p.zfar, low, p.right), (p.zright, p.zfar, high, p.left)]
        self.out, self.into = [], []
        for i, (sent, received, rows, target) in enumerate(plan):
            device = p.row(target)
            a, b = buf.at[sent, rows], buf.at[received, rows]
            self.out.append(remote(a, a, send_sems.at[i], recv_sems.at[i], device))
            self.into.append(remote(b, b, send_sems.at[i], recv_sems.at[i], device))

    def send(self, *which):
        for i in which:
            self.out[i].start()

    def arrived(self, *which):
        for i in which:
            self.into[i].wait_recv()

    def finish(self):
        for copy in self.out:
            copy.wait_send()


def gather_steps(place, gather, far_over_z, visit):
    p = place
    gather.send(0, 1, 2)
    visit(0, p.r)
    gather.arrived(0)
    gather.send(3)
    gather.arrived(1)
    gather.send(4)
    gather.arrived(2)
    gather.send(5, 6)
    visit(1, p.left)
    visit(2, p.right)
    visit(3, p.z)
    gather.arrived(3, 4)
    if far_over_z:
        gather.send(7)
    visit(4, p.far)
    gather.arrived(5)
    if not far_over_z:
        gather.send(7)
    gather.arrived(6)
    if not far_over_z:
        gather.send(8)
    visit(5, p.zleft)
    visit(6, p.zright)
    if far_over_z:
        gather.arrived(7)
    else:
        gather.arrived(7, 8)
    visit(7, p.zfar)


def order_of(p):
    return [p.r, p.left, p.right, p.z, p.far, p.zleft, p.zright, p.zfar]


def project_kernel(
    x_ref, mod_ref, w_hbm, paths_hbm, drift_hbm,
    qkv_ref, full_ref, state_hbm, moved_hbm,
    w_ref, sq_out, sq_in, part, out_part, in_part,
    w_sems, sq_sems, send_sems, recv_sems, col_send, col_recv, tm_send, tm_recv,
):
    p = Place()
    weight_copies = [
        pltpu.make_async_copy(w_hbm.at[j], w_ref.at[j], w_sems.at[j]) for j in range(3)
    ]
    for copy in weight_copies:
        copy.start()
    after = (lax.rem(p.t + 1, 8), p.r, p.c)
    before = (lax.rem(p.t + 7, 8), p.r, p.c)
    greet([p.row(p.right), p.row(p.left), p.row(p.z), p.col(), before], 5)
    squares = jnp.zeros((128, 1), F32)
    for i in range(4):
        piece = x_ref[:, i * 768 : (i + 1) * 768].astype(F32)
        squares = squares + jnp.sum(piece * piece, axis=-1, keepdims=True)
    sq_out[...] = jnp.broadcast_to(squares, (128, 128))
    swap = remote(sq_out, sq_in, sq_sems.at[0], sq_sems.at[1], p.col())
    swap.start()
    swap.wait()
    total = sq_out[:, :1] + sq_in[:, :1]
    scale = lax.rsqrt(total / D + norm_eps)
    for i in range(4):
        cols = slice(i * 768, (i + 1) * 768)
        piece = x_ref[:, cols].astype(F32)
        full_ref[p.r, :, cols] = (
            piece * scale * (1.0 + mod_ref[0:1, cols]) + mod_ref[1:2, cols]
        ).astype(BF16)

    gather = Gather(p, full_ref, send_sems, recv_sems, False)
    col_copies = []
    moves = [
        remote(paths_hbm, state_hbm, tm_send.at[0], tm_recv.at[0], after),
        remote(drift_hbm, moved_hbm, tm_send.at[1], tm_recv.at[1], after),
    ]

    def visit(k, owner):
        if k == 0:
            for move in moves:
                move.start()
            for copy in weight_copies:
                copy.wait()

        @pl.loop(0, 3)
        def _(j):
            term = jnp.dot(full_ref[owner], w_ref[j], preferred_element_type=F32)
            part[k, j] = term
            out_part[k, j] = term.astype(BF16)

        copy = remote(out_part.at[k], in_part.at[k], col_send.at[k], col_recv.at[k], p.col())
        copy.start()
        col_copies.append(copy)

    gather_steps(p, gather, False, visit)
    for k, owner in enumerate(order_of(p)):
        col_copies[k].wait_recv()
        for j in range(3):
            qkv_ref[j, owner] = (part[k, j] + in_part[k, j].astype(F32)).astype(BF16)
    for copy in col_copies:
        copy.wait_send()
    for move in moves:
        move.wait()
    gather.finish()


def project(x, mod, w, paths, drift):
    vmem = pl.BlockSpec(memory_space=pltpu.VMEM)
    hbm = pl.BlockSpec(memory_space=pl.ANY)
    dma = pltpu.SemaphoreType.DMA
    return pl.pallas_call(
        project_kernel,
        out_shape=(
            jax.ShapeDtypeStruct((3, 8, 128, 384), BF16),
            jax.ShapeDtypeStruct((8, 128, 3072), BF16),
            jax.ShapeDtypeStruct((128, 3072), BF16),
            jax.ShapeDtypeStruct((128, 3072), BF16),
        ),
        in_specs=[vmem, vmem, hbm, hbm, hbm],
        out_specs=(vmem, vmem, hbm, hbm),
        scratch_shapes=[
            pltpu.VMEM((3, 3072, 384), BF16),
            pltpu.VMEM((128, 128), F32),
            pltpu.VMEM((128, 128), F32),
            pltpu.VMEM((8, 3, 128, 384), F32),
            pltpu.VMEM((8, 3, 128, 384), BF16),
            pltpu.VMEM((8, 3, 128, 384), BF16),
            dma((3,)),
            dma((2,)),
            dma((9,)),
            dma((9,)),
            dma((8,)),
            dma((8,)),
            dma((2,)),
            dma((2,)),
        ],
        name="project",
        cost_estimate=pl.CostEstimate(
            flops=2 * 1024 * 3072 * 1152, bytes_accessed=20_000_000, transcendentals=0
        ),
        compiler_params=pltpu.CompilerParams(
            collective_id=1, has_side_effects=True, vmem_limit_bytes=VMEM_LIMIT
        ),
    )(x, mod, w, paths, drift)


def attend_kernel(
    qkv_ref, w_ref, base_ref,
    grads_ref, up_ref, mixed_ref,
    probs, outbox, inbox, half_in, gm_part, gm_out, gm_in, key_acc, value_acc,
    rs_send, rs_recv, send_sems, recv_sems, col_send, col_recv,
):
    p = Place()
    greet([p.row(p.right), p.row(p.left), p.row(p.z), p.col()], 4)

    def keys(h):
        return qkv_ref[1, :, :, h * 128 : (h + 1) * 128].reshape(1024, 128)

    def values(h):
        return qkv_ref[2, :, :, h * 128 : (h + 1) * 128].reshape(1024, 128)

    def attend(owner):
        for h in range(3):
            cols = slice(h * 128, (h + 1) * 128)
            scores = (
                lax.dot_general(
                    qkv_ref[0, owner, :, cols],
                    keys(h),
                    (((1,), (1,)), ((), ())),
                    preferred_element_type=F32,
                )
                * SCALE
            )
            top = jnp.max(scores, axis=-1, keepdims=True)
            weights = jnp.exp(scores - top)
            weights = weights * (1.0 / jnp.sum(weights, axis=-1, keepdims=True))
            probs[h, owner] = weights
            mixed_ref[owner, :, cols] = jnp.dot(
                weights.astype(BF16), values(h), preferred_element_type=F32
            ).astype(BF16)

    def out_rows(owner, lo, n, extra, put):
        @pl.loop(0, 4)
        def _(i):
            cols = pl.ds(pl.multiple_of(i * 768, 768), 768)
            term = jnp.dot(
                mixed_ref[owner, lo : lo + n, :], w_ref[:, cols], preferred_element_type=F32
            )
            for ref in extra:
                term = term + ref[:, cols].astype(F32)
            put(cols, term)

    def to_slot(slot, lo, n):
        def put(cols, term):
            outbox[slot, lo : lo + n, cols] = term.astype(BF16)

        return put

    low, high = pl.ds(0, 64), pl.ds(64, 64)
    messages = [
        (outbox.at[0], inbox.at[0], p.z),
        (outbox.at[1], inbox.at[1], p.left),
        (outbox.at[2], inbox.at[2], p.right),
        (outbox.at[3, low], half_in.at[0], p.left),
        (outbox.at[3, high], half_in.at[1], p.right),
        (outbox.at[4], inbox.at[3], p.left),
        (outbox.at[5], inbox.at[4], p.right),
        (outbox.at[6], inbox.at[5], p.z),
    ]
    copies = [
        remote(src, dst, rs_send.at[i], rs_recv.at[i], p.row(target))
        for i, (src, dst, target) in enumerate(messages)
    ]
    for slot, owner in enumerate([p.zfar, p.zleft, p.zright]):
        attend(owner)
        out_rows(owner, 0, 128, [], to_slot(slot, 0, 128))
        copies[slot].start()

    @pl.loop(0, 5)
    def _(i):
        owner = jnp.where(
            i == 0,
            p.far,
            jnp.where(i == 1, p.left, jnp.where(i == 2, p.right, jnp.where(i == 3, p.z, p.r))),
        )
        attend(owner)

    copies[0].wait_recv()
    out_rows(p.far, 0, 128, [inbox.at[0]], to_slot(3, 0, 128))
    copies[3].start()
    copies[4].start()
    copies[1].wait_recv()
    copies[2].wait_recv()
    out_rows(p.z, 0, 128, [inbox.at[1], inbox.at[2]], to_slot(6, 0, 128))
    copies[7].start()
    out_rows(p.left, 64, 64, [], to_slot(4, 64, 64))
    out_rows(p.right, 0, 64, [], to_slot(5, 0, 64))
    copies[3].wait_recv()
    out_rows(p.left, 0, 64, [half_in.at[0]], to_slot(4, 0, 64))
    copies[5].start()
    copies[4].wait_recv()
    out_rows(p.right, 64, 64, [half_in.at[1]], to_slot(5, 64, 64))
    copies[6].start()
    key_acc[...] = jnp.zeros_like(key_acc)
    value_acc[...] = jnp.zeros_like(value_acc)
    copies[5].wait_recv()
    copies[6].wait_recv()
    copies[7].wait_recv()

    def to_up(cols, term):
        up_ref[p.r, :, cols] = ((base_ref[:, cols] + term) * (1024**-0.5)).astype(BF16)

    out_rows(p.r, 0, 128, [inbox.at[3], inbox.at[4], inbox.at[5]], to_up)

    gather = Gather(p, up_ref, send_sems, recv_sems, True)
    col_copies = []
    waiting = []

    def backward(k, owner):
        col_copies[k].wait_recv()
        grad = (gm_part[k] + gm_in[k].astype(F32)).astype(BF16)
        tokens = pl.ds(pl.multiple_of(owner * 128, 128), 128)
        for h in range(3):
            cols = slice(h * 128, (h + 1) * 128)
            head_grad = grad[:, cols]
            weights = probs[h, owner]
            value_acc[h] += jnp.dot(
                head_grad.T, weights.astype(BF16), preferred_element_type=F32
            )
            grad_weights = lax.dot_general(
                head_grad, values(h), (((1,), (1,)), ((), ())), preferred_element_type=F32
            )
            inner = jnp.sum(grad_weights * weights, axis=-1, keepdims=True)
            grad_scores = (weights * (grad_weights - inner) * SCALE).astype(BF16)
            query_grad = jnp.dot(grad_scores, keys(h), preferred_element_type=F32)
            grads_ref[0, cols, tokens] = query_grad.T.astype(BF16)
            key_acc[h] += jnp.dot(
                qkv_ref[0, owner, :, cols].T, grad_scores, preferred_element_type=F32
            )

    def visit(k, owner):
        term = lax.dot_general(
            up_ref[owner], w_ref[...], (((1,), (1,)), ((), ())), preferred_element_type=F32
        )
        gm_part[k] = term
        gm_out[k] = term.astype(BF16)
        copy = remote(gm_out.at[k], gm_in.at[k], col_send.at[k], col_recv.at[k], p.col())
        copy.start()
        col_copies.append(copy)
        if waiting:
            backward(*waiting.pop())
        waiting.append((k, owner))

    gather_steps(p, gather, True, visit)
    backward(*waiting.pop())
    for h in range(3):
        cols = slice(h * 128, (h + 1) * 128)
        grads_ref[1, cols, :] = key_acc[h].astype(BF16)
        grads_ref[2, cols, :] = value_acc[h].astype(BF16)
    for copy in copies + col_copies:
        copy.wait_send()
    gather.finish()


def attend(qkv, w, base):
    vmem = pl.BlockSpec(memory_space=pltpu.VMEM)
    dma = pltpu.SemaphoreType.DMA
    return pl.pallas_call(
        attend_kernel,
        out_shape=(
            jax.ShapeDtypeStruct((3, 384, 1024), BF16),
            jax.ShapeDtypeStruct((8, 128, 3072), BF16),
            jax.ShapeDtypeStruct((8, 128, 384), BF16),
        ),
        in_specs=[vmem] * 3,
        out_specs=(vmem,) * 3,
        scratch_shapes=[
            pltpu.VMEM((3, 8, 128, 1024), F32),
            pltpu.VMEM((7, 128, 3072), BF16),
            pltpu.VMEM((6, 128, 3072), BF16),
            pltpu.VMEM((2, 64, 3072), BF16),
            pltpu.VMEM((8, 128, 384), F32),
            pltpu.VMEM((8, 128, 384), BF16),
            pltpu.VMEM((8, 128, 384), BF16),
            pltpu.VMEM((3, 128, 1024), F32),
            pltpu.VMEM((3, 128, 1024), F32),
            dma((8,)),
            dma((8,)),
            dma((8,)),
            dma((8,)),
            dma((8,)),
            dma((8,)),
        ],
        name="attend",
        cost_estimate=pl.CostEstimate(
            flops=10_000_000_000, bytes_accessed=15_000_000, transcendentals=3 * 1024 * 1024
        ),
        compiler_params=pltpu.CompilerParams(
            collective_id=2, has_side_effects=True, vmem_limit_bytes=VMEM_LIMIT
        ),
    )(qkv, w, base)


def body(paths, prev_drift, boundary, step_scale, time_ids, mod_table, w_qkv, output_weight):
    modulation = lax.dynamic_index_in_dim(mod_table, time_ids[0], 0, keepdims=False).astype(F32)
    w = jnp.transpose(w_qkv, (1, 0, 2))
    qkv, normed, moved_state, moved_drift = project(
        paths[0], modulation, w, paths[0], prev_drift[0]
    )
    at_start = lax.axis_index("tm") == 0
    prev_state = jnp.where(at_start, boundary[0], moved_state).astype(F32)
    prev_shift = jnp.where(at_start, boundary[1], moved_drift).astype(F32)
    target = prev_state + step_scale[0] * (prev_shift - prev_drift[0].astype(F32))
    base = paths[0].astype(F32) - target
    grads, upstream, mixed = attend(qkv, output_weight, base)
    grads = grads.reshape(1152, 1024)
    normed = normed.reshape(1024, 3072)
    output_gradient = lax.dot_general(
        mixed.reshape(1024, 384),
        upstream.reshape(1024, 3072),
        (((0,), (0,)), ((), ())),
        preferred_element_type=F32,
    )
    input_gradient = jnp.dot(grads, normed, preferred_element_type=F32)
    grad_in_sum = lax.psum_scatter(
        input_gradient.astype(BF16), "tm", scatter_dimension=1, tiled=True
    ).astype(F32)
    grad_in_sum = jnp.transpose(grad_in_sum.reshape(3, 384, 384), (2, 0, 1))
    grad_out_sum = lax.psum_scatter(
        output_gradient.astype(BF16), "tm", scatter_dimension=1, tiled=True
    ).astype(F32)
    return (grad_in_sum, grad_out_sum)


def solution(mesh):
    placed = (
        P("tm", "row", "col"),
        P("tm", "row", "col"),
        P(None, "row", "col"),
        P("tm"),
        P("tm"),
        P(None, None, "col"),
        P("col", None, "row"),
        P("row", "col"),
    )
    return jax.shard_map(
        body,
        mesh=mesh,
        in_specs=placed,
        out_specs=(P(("col", "tm"), None, "row"), P("row", ("col", "tm"))),
        check_vma=False,
    )
```

time: 589 us -> 322 us (0.55)
  waiting for transfers between devices: 276 us -> 56.9 us
  Pallas kernels: 0 us -> 206 us
  blocking collectives: 121 us -> 0 us
  matrix products: 88.7 us -> 17.8 us
  other arithmetic: 33.4 us -> 5.43 us
  local copies, waits for them, and re-layouts: 45.3 us -> 19.1 us
  starting transfers between devices: 7.54 us -> 0.08 us
    pallas_call x0 -> x2, Pallas kernels: none -> 206 us  [the longest x1 125 us: attend(): pl.pallas_call(attend_kernel, out_shape=(jax.ShapeDtypeStruct((3, 384, 10...]
    all_gather x2 -> x0, waiting for transfers between devices: 136 us -> none  [the longest x1 71.1 us: body(): slice_rows = lax.all_gather(upstream, 'row', axis=1, tiled=True)]
    psum x2 -> x0, blocking collectives: 121 us -> none  [the longest x1 114 us: body(): projected = lax.psum(partial_query_key_value, 'col').astype(jnp.bfloat16)]
    reduce_scatter x2 -> x0, waiting for transfers between devices: 91.6 us -> none  [the longest x1 48.6 us: body(): lax.psum_scatter(jnp.einsum('lsh,hd->lsd', attention_block, output_weight...]
    dot_general x24 -> x2, matrix products: 88.7 us -> 17.8 us  [the longest x1 12.1 us: body(): input_gradient = jnp.dot(grads, normed, preferred_element_type=F32)]
    unnamed x7 -> x4, waiting for transfers between devices: 0.12 us -> 56.9 us
    psum x1 -> x0, waiting for transfers between devices: 33.1 us -> none  [body(): grad_mixed = lax.psum(grad_partial.astype(jnp.bfloat16), 'col')]
    convert_element_type x7 -> x2, other arithmetic: 19.9 us -> 2.19 us  [the longest x1 1.33 us: body(): lax.dynamic_index_in_dim(mod_table, time_ids[0], 0, keepdims=False)]
  transfers between devices with their start and end apart: 8 -> 2, of which waited for: 7 -> 2; matrix products, arithmetic and copies ran while one was open for 14% -> 7% of each run, Pallas kernels for 0% -> 0%
where the time goes in v1:
time: 322 us; the launch traced here: 321 us
  Pallas kernels  206 us (64%)
  waiting for transfers between devices  56.9 us (18%)
  local copies, waits for them, and re-layouts  19.1 us (6%)
  matrix products  17.8 us (6%)
  between operations  15.4 us (5%)
  other arithmetic  5.43 us (2%)
    pallas_call x1, Pallas kernels, attend(): pl.pallas_call(attend_kernel, out_shape=(jax.ShapeDtypeStruct((3, 384, 10...  125 us
    pallas_call x1, Pallas kernels, project(): pl.pallas_call(project_kernel, out_shape=(jax.ShapeDtypeStruct((3, 8, 128...  81.3 us
    unnamed x4, waiting for transfers between devices  56.9 us
    unnamed x12, local copies, waits for them, and re-layouts  16.7 us
    dot_general x1, matrix products, body(): input_gradient = jnp.dot(grads, normed, preferred_element_type=F32)  12.1 us
  transfers between devices with their start and end apart: 2, of which 2 were waited for; matrix products, arithmetic and copies ran while one was open for 7% of the time, Pallas kernels for 0%

profile of v1, /device:TPU:1, one launch (start us, length us, event | category | flops | bytes accessed | tf_op | source)
XLA Modules:
  0.0 321.2 jit_solution(3253626026414016772)
XLA Ops:
  7.2 0.0 reduce-scatter.9.cloned.1.call-start
  8.5 1.3 bitcast_convert_fusion.1.mod_ref
  9.8 0.0 copy-start
  9.8 0.0 copy-start.1
  9.8 0.0 copy-start.2
  9.8 81.3 %project.1 = (bf16[3,8,128,384]{3,2,1,0:T(8,128)(2,1)}, bf16[8,128,3072]{2,1,0:T(8,128)(2,1)}, bf16[128,3072]{1,0:T(8,128)(2,1)}, bf16[128,3072]{1,0:T(8,128)(2,1)}) custom-call(bf16[128,3072]{1,0:T(8,128)(2,1)} %bitcast.42, f32[2,3072]{1,0:T(2,128)} %bitcast_convert_fusion.1.mod_ref, bf16[3,3072,384]{2,1,0:T(8,128)(2,1)} %bitcast.46, ...), custom_call_target="tpu_custom_call" | custom-call | flops 7247757312 | bytes 20000000 | tf_op jit(solution)/shard_map/project/pallas_call | solution.py:206
  91.1 0.0 copy-done
  91.2 0.0 copy-done.1
  91.2 0.0 copy-done.2
  91.2 3.2 %add_subtract_fusion.base_ref = f32[128,3072]{1,0:T(8,128)} fusion(bf16[128,3072]{1,0:T(8,128)(2,1)} %get-tuple-element.11, bf16[128,3072]{1,0:T(8,128)(2,1)} %get-tuple-element.10, bf16[2,128,3072]{2,1,0:T(8,128)(2,1)S(1)} %copy-done, f32[]{:T(128)} %bitcast.33, pred[]{:T(512)S(6)} %eq.3, bf16[1,128,3072]{2,1,0:T(8,128)(2,1)S(1)} %copy-done.2, ...), kind=kLoop, calls=%fused_computation.2 | loop fusion | flops 3932160 | bytes 6291461 | tf_op jit(solution)/shard_map/sub | solution.py:449
  94.4 125.2 %attend.1 = (bf16[3,384,1024]{2,1,0:T(8,128)(2,1)}, bf16[8,128,3072]{2,1,0:T(8,128)(2,1)}, bf16[8,128,384]{2,1,0:T(8,128)(2,1)}) custom-call(bf16[3,8,128,384]{3,2,1,0:T(8,128)(2,1)} %get-tuple-element.9.qkv_ref, bf16[384,3072]{1,0:T(8,128)(2,1)} %w_ref.1, f32[128,3072]{1,0:T(8,128)} %add_subtract_fusion.base_ref), custom_call_target="tpu_custom_call" | custom-call | flops 10000000000 | bytes 15000000 | tf_op jit(solution)/shard_map/attend/pallas_call | solution.py:403
  219.6 5.7 %bitcast_convert_fusion = bf16[384,3072]{1,0:T(8,128)(2,1)S(1)} fusion(bf16[8,128,384]{2,1,0:T(8,128)(2,1)} %get-tuple-element.14, bf16[8,128,3072]{2,1,0:T(8,128)(2,1)} %get-tuple-element.15), kind=kOutput, calls=%fused_computation.1 | convolution fusion | flops 2417098752 | bytes 9437184 | tf_op jit(solution)/shard_map/dot_general | solution.py:453
  225.3 2.5 copy.17
  227.8 0.0 copy-start.3
  227.8 0.0 reduce-scatter.9.cloned.1.call-update
  227.8 0.0 reduce-scatter.7.cloned.1.call-start
  227.9 1.6 copy-done.3
  229.5 12.1 %convolution_convert_fusion = bf16[1152,3072]{1,0:T(8,128)(2,1)} fusion(bf16[1152,1024]{1,0:T(8,128)(2,1)S(1)} %bitcast.48, bf16[1024,3072]{1,0:T(8,128)(2,1)} %bitcast.47), kind=kOutput, calls=%fused_computation | convolution fusion | flops 7251296256 | bytes 15728640 | tf_op jit(solution)/shard_map/dot_general | solution.py:459
  241.6 9.8 %copy.15 = bf16[1152,3072]{0,1:T(8,128)(2,1)} copy(bf16[1152,3072]{1,0:T(8,128)(2,1)} %convolution_convert_fusion) | data formatting | bytes 14155776
  251.3 0.0 reduce-scatter.7.cloned.1.call-update
  251.4 9.0 %reduce-scatter.9.cloned.1.call-done = bf16[384,384]{1,0:T(8,128)(2,1)} async-done(((bf16[3072,384]{1,0:T(8,128)(2,1)}), bf16[384,384]{1,0:T(8,128)(2,1)}) %reduce-scatter.9.cloned.1.call-update) | async-done | bytes 294928
  260.3 1.2 copy.18
  261.5 0.9 convert_element_type.35
  262.4 47.9 %reduce-scatter.7.cloned.1.call-done = bf16[384,1152]{1,0:T(8,128)(2,1)} async-done(((bf16[3072,1152]{1,0:T(8,128)(2,1)}), bf16[384,1152]{1,0:T(8,128)(2,1)}) %reduce-scatter.7.cloned.1.call-update) | async-done | bytes 884752
  310.3 1.7 copy.16
  312.0 2.4 copy.12
Async XLA Ops:
  7.2 253.2 %reduce-scatter.9.cloned.1.call-start = ((), (), s32[]{:S(2)}) async-start(), calls=%async_computation.3 | async-start | bytes 2654208
  9.8 81.3 %copy-start = (bf16[2,128,3072]{2,1,0:T(8,128)(2,1)S(1)}, bf16[2,128,3072]{2,1,0:T(8,128)(2,1)}, u32[]{:S(2)}) copy-start(bf16[2,128,3072]{2,1,0:T(8,128)(2,1)} %param.10) | copy-start | bytes 4718596
  9.8 81.3 %copy-start.1 = (bf16[1,128,3072]{2,1,0:T(8,128)(2,1)S(1)}, bf16[1,128,3072]{2,1,0:T(8,128)(2,1)}, u32[]{:S(2)}) copy-start(bf16[1,128,3072]{2,1,0:T(8,128)(2,1)} %param.8) | copy-start | bytes 2359300
  9.8 81.3 %copy-start.2 = (bf16[1,128,3072]{2,1,0:T(8,128)(2,1)S(1)}, bf16[1,128,3072]{2,1,0:T(8,128)(2,1)}, u32[]{:S(2)}) copy-start(bf16[1,128,3072]{2,1,0:T(8,128)(2,1)} %param.9) | copy-start | bytes 2359300
  227.8 1.7 copy-start.3
  227.8 82.4 %reduce-scatter.7.cloned.1.call-start = ((), (), s32[]{:S(2)}) async-start(), calls=%async_computation.2 | async-start | bytes 7962624
Sparse Core Ops, SparseCore 0:
  227.9 32.3 reduce-scatter.8
  262.8 47.4 reduce-scatter.6

commit v2 on v1

--- a/solution.py
+++ b/solution.py
@@ -436,6 +436,173 @@
     )(qkv, w, base)
 
 
+def reduce_kernel(
+    grads_ref, mixed_ref, normed_hbm, up_hbm,
+    in_ref, out_ref,
+    mixed_t, normed, up, core_out, core_in, y_out, y_in, left_low, right_high, own,
+    normed_sems, up_sems, core_send, core_recv, y_send, y_recv,
+):
+    p = Place()
+    core = lax.rem(p.t, 2)
+    y = p.t // 2
+    peers = [lax.rem(y + by, 4) for by in (2, 3, 1, 0)]
+    theirs = [2 * peer + 1 - core for peer in peers]
+    mine = [2 * peer + core for peer in peers]
+    order = [
+        theirs[0], theirs[1], mine[0], theirs[2], mine[1], theirs[3], mine[2], mine[3],
+    ]
+    loads = []
+    for k, owner in enumerate(order):
+        cols = pl.ds(pl.multiple_of(owner * 384, 384), 384)
+        loads.append(
+            (
+                pltpu.make_async_copy(normed_hbm.at[:, :, cols], normed.at[k], normed_sems.at[k]),
+                pltpu.make_async_copy(up_hbm.at[:, :, cols], up.at[k], up_sems.at[k]),
+            )
+        )
+        for copy in loads[-1]:
+            copy.start()
+    partner = (2 * y + 1 - core, p.r, p.c)
+    to_left = (2 * peers[1] + core, p.r, p.c)
+    to_right = (2 * peers[2] + core, p.r, p.c)
+    greet([partner, to_left, to_right], 3)
+    mixed_t[...] = mixed_ref[...].reshape(1024, 384).T
+
+    def chunk(k, put):
+        for copy in loads[k]:
+            copy.wait()
+
+        @pl.loop(0, 3)
+        def _(j):
+            put(
+                j,
+                jnp.dot(
+                    grads_ref[j], normed[k].reshape(1024, 384), preferred_element_type=F32
+                ),
+            )
+
+        put(3, jnp.dot(mixed_t[...], up[k].reshape(1024, 384), preferred_element_type=F32))
+
+    core_copies = [
+        remote(core_out.at[i], core_in.at[i], core_send.at[i], core_recv.at[i], partner)
+        for i in range(4)
+    ]
+    low, high = pl.ds(0, 2), pl.ds(2, 2)
+    messages = [
+        (y_out.at[0, low], to_left),
+        (y_out.at[0, high], to_right),
+        (y_out.at[1, high], to_left),
+        (y_out.at[2, low], to_right),
+        (y_out.at[1, low], to_left),
+        (y_out.at[2, high], to_right),
+    ]
+    y_copies = [
+        remote(src, y_in.at[i], y_send.at[i], y_recv.at[i], device)
+        for i, (src, device) in enumerate(messages)
+    ]
+
+    def for_partner(k, i):
+        def put(j, term):
+            core_out[i, j] = term.astype(BF16)
+
+        chunk(k, put)
+        core_copies[i].start()
+
+    def for_far(j, term):
+        y_out[0, j] = (term + core_in[0, j].astype(F32)).astype(BF16)
+
+    def for_left(j, term):
+        total = term + core_in[1, j].astype(F32)
+        y_out[1, j] = total.astype(BF16)
+        left_low[j] = total
+
+    def for_right(j, term):
+        total = term + core_in[2, j].astype(F32)
+        y_out[2, j] = total.astype(BF16)
+        right_high[j] = total
+
+    def for_own(j, term):
+        own[j] = term + core_in[3, j].astype(F32)
+
+    for_partner(0, 0)
+    for_partner(1, 1)
+    core_copies[0].wait_recv()
+    chunk(2, for_far)
+    y_copies[0].start()
+    y_copies[1].start()
+    for_partner(3, 2)
+    core_copies[1].wait_recv()
+    chunk(4, for_left)
+    y_copies[2].start()
+    for_partner(5, 3)
+    core_copies[2].wait_recv()
+    chunk(6, for_right)
+    y_copies[3].start()
+    core_copies[3].wait_recv()
+    chunk(7, for_own)
+    y_copies[0].wait_recv()
+    for j in (0, 1):
+        y_out[1, j] = (left_low[j] + y_in[0, j].astype(F32)).astype(BF16)
+    y_copies[4].start()
+    y_copies[1].wait_recv()
+    for j in (2, 3):
+        y_out[2, j] = (right_high[j] + y_in[1, j - 2].astype(F32)).astype(BF16)
+    y_copies[5].start()
+    y_copies[2].wait_recv()
+    y_copies[3].wait_recv()
+    for j in (0, 1):
+        own[j] += y_in[3, j].astype(F32)
+        own[j + 2] += y_in[2, j].astype(F32)
+    y_copies[4].wait_recv()
+    for j in (0, 1):
+        in_ref[j] = own[j] + y_in[4, j].astype(F32)
+    y_copies[5].wait_recv()
+    in_ref[2] = own[2] + y_in[5, 0].astype(F32)
+    out_ref[...] = own[3] + y_in[5, 1].astype(F32)
+    for copy in core_copies + y_copies:
+        copy.wait_send()
+
+
+def reduce(grads, mixed, normed, up):
+    vmem = pl.BlockSpec(memory_space=pltpu.VMEM)
+    hbm = pl.BlockSpec(memory_space=pl.ANY)
+    dma = pltpu.SemaphoreType.DMA
+    return pl.pallas_call(
+        reduce_kernel,
+        out_shape=(
+            jax.ShapeDtypeStruct((3, 384, 384), F32),
+            jax.ShapeDtypeStruct((384, 384), F32),
+        ),
+        in_specs=[vmem, vmem, hbm, hbm],
+        out_specs=(vmem, vmem),
+        scratch_shapes=[
+            pltpu.VMEM((384, 1024), BF16),
+            pltpu.VMEM((8, 8, 128, 384), BF16),
+            pltpu.VMEM((8, 8, 128, 384), BF16),
+            pltpu.VMEM((4, 4, 384, 384), BF16),
+            pltpu.VMEM((4, 4, 384, 384), BF16),
+            pltpu.VMEM((3, 4, 384, 384), BF16),
+            pltpu.VMEM((6, 2, 384, 384), BF16),
+            pltpu.VMEM((4, 384, 384), F32),
+            pltpu.VMEM((4, 384, 384), F32),
+            pltpu.VMEM((4, 384, 384), F32),
+            dma((8,)),
+            dma((8,)),
+            dma((4,)),
+            dma((4,)),
+            dma((6,)),
+            dma((6,)),
+        ],
+        name="reduce",
+        cost_estimate=pl.CostEstimate(
+            flops=2 * 1024 * 3072 * 1536, bytes_accessed=20_000_000, transcendentals=0
+        ),
+        compiler_params=pltpu.CompilerParams(
+            collective_id=3, has_side_effects=True, vmem_limit_bytes=VMEM_LIMIT
+        ),
+    )(grads, mixed, normed, up)
+
+
 def body(paths, prev_drift, boundary, step_scale, time_ids, mod_table, w_qkv, output_weight):
     modulation = lax.dynamic_index_in_dim(mod_table, time_ids[0], 0, keepdims=False).astype(F32)
     w = jnp.transpose(w_qkv, (1, 0, 2))
@@ -448,22 +615,8 @@
     target = prev_state + step_scale[0] * (prev_shift - prev_drift[0].astype(F32))
     base = paths[0].astype(F32) - target
     grads, upstream, mixed = attend(qkv, output_weight, base)
-    grads = grads.reshape(1152, 1024)
-    normed = normed.reshape(1024, 3072)
-    output_gradient = lax.dot_general(
-        mixed.reshape(1024, 384),
-        upstream.reshape(1024, 3072),
-        (((0,), (0,)), ((), ())),
-        preferred_element_type=F32,
-    )
-    input_gradient = jnp.dot(grads, normed, preferred_element_type=F32)
-    grad_in_sum = lax.psum_scatter(
-        input_gradient.astype(BF16), "tm", scatter_dimension=1, tiled=True
-    ).astype(F32)
-    grad_in_sum = jnp.transpose(grad_in_sum.reshape(3, 384, 384), (2, 0, 1))
-    grad_out_sum = lax.psum_scatter(
-        output_gradient.astype(BF16), "tm", scatter_dimension=1, tiled=True
-    ).astype(F32)
+    grad_in_sum, grad_out_sum = reduce(grads, mixed, normed, upstream)
+    grad_in_sum = jnp.transpose(grad_in_sum, (2, 0, 1))
     return (grad_in_sum, grad_out_sum)
 
 

time: 322 us -> 275 us (0.85)
  Pallas kernels: 206 us -> 265 us
  waiting for transfers between devices: 56.9 us -> 0 us
  matrix products: 17.8 us -> 0 us
  local copies, waits for them, and re-layouts: 19.1 us -> 3.74 us
  between operations: 15.4 us -> 1.99 us
    pallas_call x0 -> x1, Pallas kernels: none -> 58.3 us  [reduce(): pl.pallas_call(reduce_kernel, out_shape=(jax.ShapeDtypeStruct((3, 384, 38...]
    unnamed x4 -> x0, waiting for transfers between devices: 56.9 us -> none
    dot_general x2 -> x0, matrix products: 17.8 us -> none  [the longest x1 12.1 us: body(): input_gradient = jnp.dot(grads, normed, preferred_element_type=F32)]
    unnamed x12 -> x10, local copies, waits for them, and re-layouts: 16.7 us -> 3.74 us
  transfers between devices with their start and end apart: 2 -> 0, of which waited for: 2 -> 0; matrix products, arithmetic and copies ran while one was open for 7% -> 0% of each run, Pallas kernels for 0% -> 0%
where the time goes in v2:
time: 275 us
  Pallas kernels  265 us (96%)
  other arithmetic  4.58 us (2%)
  local copies, waits for them, and re-layouts  3.74 us (1%)
    pallas_call x1, Pallas kernels, attend(): pl.pallas_call(attend_kernel, out_shape=(jax.ShapeDtypeStruct((3, 384, 10...  125 us
    pallas_call x1, Pallas kernels, project(): pl.pallas_call(project_kernel, out_shape=(jax.ShapeDtypeStruct((3, 8, 128...  81.3 us
    pallas_call x1, Pallas kernels, reduce(): pl.pallas_call(reduce_kernel, out_shape=(jax.ShapeDtypeStruct((3, 384, 38...  58.3 us

profile of v2, /device:TPU:1, one launch (start us, length us, event | category | flops | bytes accessed | tf_op | source)
XLA Modules:
  0.0 275.0 jit_solution(16478065498058478302)
XLA Ops:
  1.9 1.3 bitcast_convert_fusion.mod_ref
  3.3 0.0 copy-start
  3.3 0.0 copy-start.1
  3.3 0.0 copy-start.2
  3.3 81.3 %project.1 = (bf16[3,8,128,384]{3,2,1,0:T(8,128)(2,1)}, bf16[8,128,3072]{2,1,0:T(8,128)(2,1)}, bf16[128,3072]{1,0:T(8,128)(2,1)}, bf16[128,3072]{1,0:T(8,128)(2,1)}) custom-call(bf16[128,3072]{1,0:T(8,128)(2,1)} %bitcast.24, f32[2,3072]{1,0:T(2,128)} %bitcast_convert_fusion.mod_ref, bf16[3,3072,384]{2,1,0:T(8,128)(2,1)} %bitcast.27, ...), custom_call_target="tpu_custom_call" | custom-call | flops 7247757312 | bytes 20000000 | tf_op jit(solution)/shard_map/project/pallas_call | solution.py:206
  84.6 0.0 copy-done
  84.6 0.0 copy-done.1
  84.6 0.0 copy-done.2
  84.6 3.2 %add_subtract_fusion.base_ref = f32[128,3072]{1,0:T(8,128)} fusion(bf16[128,3072]{1,0:T(8,128)(2,1)} %get-tuple-element.13, bf16[128,3072]{1,0:T(8,128)(2,1)} %get-tuple-element.12, bf16[2,128,3072]{2,1,0:T(8,128)(2,1)S(1)} %copy-done, f32[]{:T(128)} %bitcast.19, pred[]{:T(512)S(6)} %eq.3, bf16[1,128,3072]{2,1,0:T(8,128)(2,1)S(1)} %copy-done.2, ...), kind=kLoop, calls=%fused_computation | loop fusion | flops 3932160 | bytes 6291461 | tf_op jit(solution)/shard_map/sub | solution.py:616
  87.8 125.1 %attend.1 = (bf16[3,384,1024]{2,1,0:T(8,128)(2,1)}, bf16[8,128,3072]{2,1,0:T(8,128)(2,1)}, bf16[8,128,384]{2,1,0:T(8,128)(2,1)}) custom-call(bf16[3,8,128,384]{3,2,1,0:T(8,128)(2,1)} %get-tuple-element.11.qkv_ref, bf16[384,3072]{1,0:T(8,128)(2,1)} %w_ref.1, f32[128,3072]{1,0:T(8,128)} %add_subtract_fusion.base_ref), custom_call_target="tpu_custom_call" | custom-call | flops 10000000000 | bytes 15000000 | tf_op jit(solution)/shard_map/attend/pallas_call | solution.py:403
  212.9 58.3 %reduce.1 = (f32[3,384,384]{2,1,0:T(8,128)}, f32[384,384]{1,0:T(8,128)}) custom-call(bf16[3,384,1024]{2,1,0:T(8,128)(2,1)} %get-tuple-element.14.grads_ref, bf16[8,128,384]{2,1,0:T(8,128)(2,1)} %get-tuple-element.15.mixed_ref, bf16[8,128,3072]{2,1,0:T(8,128)(2,1)} %get-tuple-element.16.normed_hbm, bf16[8,128,3072]{2,1,0:T(8,128)(2,1)} %get-tuple-element.17.up_hbm), custom_call_target="tpu_custom_call" | custom-call | flops 9663676416 | bytes 20000000 | tf_op jit(solution)/shard_map/reduce/pallas_call | solution.py:570
  271.2 0.0 copy-start.3
  271.2 2.9 %copy.10 = f32[384,3,384]{2,0,1:T(8,128)} copy(f32[384,3,384]{0,2,1:T(8,128)} %bitcast.23) | data formatting | bytes 3538944
  274.2 0.0 copy-done.3
  274.2 0.8 copy.14
Async XLA Ops:
  3.3 81.3 %copy-start = (bf16[2,128,3072]{2,1,0:T(8,128)(2,1)S(1)}, bf16[2,128,3072]{2,1,0:T(8,128)(2,1)}, u32[]{:S(2)}) copy-start(bf16[2,128,3072]{2,1,0:T(8,128)(2,1)} %param.10) | copy-start | bytes 4718596
  3.3 81.3 %copy-start.1 = (bf16[1,128,3072]{2,1,0:T(8,128)(2,1)S(1)}, bf16[1,128,3072]{2,1,0:T(8,128)(2,1)}, u32[]{:S(2)}) copy-start(bf16[1,128,3072]{2,1,0:T(8,128)(2,1)} %param.8) | copy-start | bytes 2359300
  3.3 81.3 %copy-start.2 = (bf16[1,128,3072]{2,1,0:T(8,128)(2,1)S(1)}, bf16[1,128,3072]{2,1,0:T(8,128)(2,1)}, u32[]{:S(2)}) copy-start(bf16[1,128,3072]{2,1,0:T(8,128)(2,1)} %param.9) | copy-start | bytes 2359300
  271.2 2.9 %copy-start.3 = (f32[384,384]{1,0:T(8,128)S(1)}, f32[384,384]{1,0:T(8,128)}, u32[]{:S(2)}) copy-start(f32[384,384]{1,0:T(8,128)} %get-tuple-element.25) | copy-start | bytes 1769476
